TPU v7x, 32 devices: a whole 2x2x4 slice. The times are simulated.
32 devices in a mesh: groups: 2 (over y), wide: 4 (over z), narrow: 2 (over x), lev: 2 (over core).
Axes of the slice: x: 2, y: 2, z: 4, core: 2. Of those that a mesh axis runs over, the one named last changes fastest.
Arguments:
- parent_state: float32 [2, 64, 128, 256], P(None, 'lev', ('groups', 'wide'), 'narrow'), parts along dimension 2, may hold values from -6 to 6
- nest_state: float32 [2, 64, 64, 512], P(None, 'lev', ('groups', 'wide'), 'narrow'), parts along dimension 2, may hold values from -6 to 6
- level_weights: float32 [64], P('lev'), may hold values from -0.75 to 0.75
- diffusion: float32 [64], P('lev'), may hold values from 0.02 to 0.06
- smoothing: float32 [64], P('lev'), may hold values from 0.0008 to 0.0024
- coupling: float32 [64], P('lev'), may hold values from 0.02 to 0.06
- transport: float32 [64], P('lev'), may hold values from 0.1 to 0.3
- nest_anchor: int32 [2], P('groups'), parts along dimension 0, may hold values from 1 to 47
Outputs:
- parent_out: float32 [2, 64, 128, 256], P(None, 'lev', ('groups', 'wide'), 'narrow'), parts along dimension 2
- nest_out: float32 [2, 64, 64, 512], P(None, 'lev', ('groups', 'wide'), 'narrow'), parts along dimension 2
There are 2 independent parts, one for each index of `groups`. A program takes and returns all parts, laid end to end along the dimension named above; an argument that names none is the same for every part. Nothing has to cross between parts.
Inputs may be any that keep to these rules, and one draw needn't show every extreme that they name: `nest_anchor`: the rows just outside the nest on both sides lie inside the parent grid.
All inputs are finite; a program needn't handle non-finite values.
Results may differ from a plain program's by a relative error of at most 0.00002.
Values sent between devices are 32-bit elements; how exact they have to be, the bound alone decides.
A program may use at most 64 MiB of HBM per device.

v0:
```python
import jax
import jax.numpy as jnp
from jax import lax
from jax.sharding import PartitionSpec as P


def padded(cells, sides, width):
    for axis, dim in sides:
        count = lax.axis_size(axis)
        head = lax.slice_in_dim(cells, 0, width, axis=dim)
        tail = lax.slice_in_dim(cells, cells.shape[dim] - width, cells.shape[dim], axis=dim)
        cells = jnp.concatenate(
            [
                lax.ppermute(tail, axis, [(i, (i + 1) % count) for i in range(count)]),
                cells,
                lax.ppermute(head, axis, [((i + 1) % count, i) for i in range(count)]),
            ],
            axis=dim,
        )
    return cells


def laplace(values):
    return (
        values[..., 2:, 1:-1]
        + values[..., :-2, 1:-1]
        + values[..., 1:-1, 2:]
        + values[..., 1:-1, :-2]
        - 4.0 * values[..., 1:-1, 1:-1]
    )


def central(values, direction):
    if direction == 0:
        return 0.5 * (values[..., 3:-1, 2:-2] - values[..., 1:-3, 2:-2])
    return 0.5 * (values[..., 2:-2, 3:-1] - values[..., 2:-2, 1:-3])


def column_part(extended, level_weights):
    return jnp.sum(level_weights[:, None, None] * extended[0], axis=0)


def advance(extended, column, coefficients):
    diffuse = coefficients[0][:, None, None]
    smooth = coefficients[1][:, None, None]
    couple = coefficients[2][:, None, None]
    advect = coefficients[3][:, None, None]
    height = extended[0]
    tracer = extended[1]
    lap_height = laplace(height)
    new_height = (
        height[:, 2:-2, 2:-2]
        + diffuse * lap_height[:, 1:-1, 1:-1]
        - smooth * laplace(lap_height)
        + couple * laplace(column)[1:-1, 1:-1]
    )
    drift_term = central(column, 0) * central(tracer, 0) + central(column, 1) * central(tracer, 1)
    new_tracer = (
        tracer[:, 2:-2, 2:-2] + diffuse * laplace(tracer)[:, 1:-1, 1:-1] - advect * drift_term
    )
    return jnp.stack([new_height, new_tracer])


def clear_poles(extended, width, position, wide_count):
    row_index = jnp.arange(extended.shape[2], dtype=jnp.int32)
    outside = (row_index < width) & (position == 0) | (row_index >= extended.shape[2] - width) & (
        position == wide_count - 1
    )
    return jnp.where(outside[:, None], 0.0, extended)


def set_edges(extended, width, cycle_edges, position, wide_count):
    row_index = jnp.arange(extended.shape[2], dtype=jnp.int32)
    first_col = 4 - width
    col_span = extended.shape[3]
    fine_edges = jnp.repeat(cycle_edges, 2, axis=-1)[..., first_col : first_col + col_span]
    top_rows = (row_index < width) & (position == 0)
    bottom = (row_index >= extended.shape[2] - width) & (position == wide_count - 1)
    extended = jnp.where(top_rows[:, None], fine_edges[0][:, :, None, :], extended)
    return jnp.where(bottom[:, None], fine_edges[1][:, :, None, :], extended)


def cycle_rows(fields, anchor, band_rows, position):
    block_rows = fields.shape[2]
    picked_rows = []
    for global_row in (anchor - 1, anchor + band_rows):
        local_row = jnp.clip(global_row - position * block_rows, 0, block_rows - 1)
        picked_row = lax.dynamic_index_in_dim(fields, local_row, 2, keepdims=False)
        picked_rows.append(jnp.where(global_row // block_rows == position, picked_row, 0.0))
    return jnp.stack(picked_rows)


def absorb(carried, pieces, offset):
    row_index = jnp.arange(carried.shape[2], dtype=jnp.int32) + offset
    inside = (row_index >= 0) & (row_index < pieces.shape[2])
    picked_rows = jnp.take(pieces, jnp.clip(row_index, 0, pieces.shape[2] - 1), axis=2)
    return jnp.where(inside[:, None], picked_rows, carried)


def shards(
    parent_state, nest_state, level_weights, diffusion, smoothing, coupling, transport, nest_anchor
):
    wide_count = lax.axis_size("wide")
    position = lax.axis_index("wide")
    anchor = nest_anchor[0]
    band_rows = nest_state.shape[2] * wide_count // 2
    coarse_coefficients = (diffusion, smoothing, coupling, transport)
    fine_coefficients = (2.0 * diffusion, 8.0 * smoothing, 2.0 * coupling, 2.0 * transport)
    parent_ext, nest_ext = (
        padded(parent_state, (("wide", 2), ("narrow", 3)), 2),
        padded(nest_state, (("wide", 2), ("narrow", 3)), 2),
    )
    halo_depth = 2
    parent_ext = clear_poles(parent_ext, 2, position, wide_count)

    def nest_step(extended, width, cycle_edges):
        extended = set_edges(extended, width, cycle_edges, position, wide_count)
        nest_column = lax.psum(column_part(extended, level_weights), "lev")
        return advance(extended, nest_column, fine_coefficients)

    parent_column = lax.psum(column_part(parent_ext, level_weights), "lev")
    parent_new = advance(parent_ext, parent_column, coarse_coefficients)
    cycle_old, cycle_new = lax.psum(
        (
            cycle_rows(parent_state, anchor, band_rows, position),
            cycle_rows(parent_new, anchor, band_rows, position),
        ),
        "wide",
    )
    cycle_old, cycle_new = (
        padded(cycle_old, (("narrow", 3),), 2),
        padded(cycle_new, (("narrow", 3),), 2),
    )
    nest_mid = nest_step(nest_ext, halo_depth, cycle_old)
    cycle_mid = 0.5 * (cycle_old + cycle_new)
    second = padded(nest_mid, (("wide", 2), ("narrow", 3)), 2)
    nest_out = nest_step(second, 2, cycle_mid)
    coarse = 0.25 * (
        nest_out[:, :, 0::2, 0::2]
        + nest_out[:, :, 1::2, 0::2]
        + nest_out[:, :, 0::2, 1::2]
        + nest_out[:, :, 1::2, 1::2]
    )
    offset = position * parent_state.shape[2] - anchor
    parent_out = absorb(parent_new, lax.all_gather(coarse, "wide", axis=2, tiled=True), offset)
    return (parent_out, nest_out)


def solution(mesh):
    return jax.shard_map(
        shards,
        mesh=mesh,
        in_specs=(
            P(None, "lev", ("groups", "wide"), "narrow"),
            P(None, "lev", ("groups", "wide"), "narrow"),
            P("lev"),
            P("lev"),
            P("lev"),
            P("lev"),
            P("lev"),
            P("groups"),
        ),
        out_specs=(
            P(None, "lev", ("groups", "wide"), "narrow"),
            P(None, "lev", ("groups", "wide"), "narrow"),
        ),
        check_vma=False,
    )
```

profile of v0, /device:TPU:0, one launch (start us, length us, event | category | flops | bytes accessed | tf_op | source)
XLA Modules:
  0.0 183.3 jit_solution(6214573029391717680)
XLA Ops:
  7.3 1.1 fusion.68
  8.4 3.1 %collective-permute-start.2 = (f32[2,32,2,128]{3,1,2,0:T(8,128)S(1)}, f32[2,32,2,128]{3,1,2,0:T(8,128)S(1)}, u32[]{:S(2)}, u32[]{:S(2)}) collective-permute-start(f32[2,32,2,128]{3,1,2,0:T(8,128)S(1)} %copy.57), channel_id=1, source_target_pairs={{0,4},{4,8},{8,12},{12,0},{1,5},{5,9},{9,13},{13,1},{2,6},{6,10},{... | collective-permute-start | bytes 196616 | tf_op jit(solution)/shard_map/ppermute | solution.py:14
  11.5 2.1 %collective-permute-start.3 = (f32[2,32,2,128]{3,1,2,0:T(8,128)S(1)}, f32[2,32,2,128]{3,1,2,0:T(8,128)S(1)}, u32[]{:S(2)}, u32[]{:S(2)}) collective-permute-start(f32[2,32,2,128]{3,1,2,0:T(8,128)S(1)} %copy.58), channel_id=1, source_target_pairs={{4,0},{8,4},{12,8},{0,12},{5,1},{9,5},{13,9},{1,13},{6,2},{10,6},{... | collective-permute-start | bytes 196616 | tf_op jit(solution)/shard_map/ppermute | solution.py:16
  13.6 1.4 fusion.67
  15.1 3.9 %collective-permute-start.9 = (f32[2,32,2,256]{3,1,2,0:T(8,128)S(1)}, f32[2,32,2,256]{3,1,2,0:T(8,128)S(1)}, u32[]{:S(2)}, u32[]{:S(2)}) collective-permute-start(f32[2,32,2,256]{3,1,2,0:T(8,128)S(1)} %copy.60), channel_id=1, source_target_pairs={{4,0},{8,4},{12,8},{0,12},{5,1},{9,5},{13,9},{1,13},{6,2},{10,6},{... | collective-permute-start | bytes 393224 | tf_op jit(solution)/shard_map/ppermute | solution.py:16
  19.8 0.6 pad_maximum_fusion.6
  20.7 0.2 fusion.64
  20.9 0.3 copy.37
  21.2 1.7 collective-permute-start.4
  22.9 0.3 copy.38
  23.2 0.4 collective-permute-start.5
  23.7 1.6 collective-permute-done.4
  25.3 0.3 copy.39
  25.6 1.6 collective-permute-done.5
  27.3 0.3 copy.40
  27.6 0.6 maximum_select_fusion
  28.3 0.6 copy-done.4
  29.0 3.4 %psum.36 = f32[20,132]{1,0:T(8,128)S(1)} all-reduce(f32[20,132]{1,0:T(8,128)S(1)} %multiply_reduce_fusion), channel_id=1, replica_groups=mesh['groups'=2,'wide'=4,'narrow'=2,'lev'=2] {'lev'}, use_global_device_ids=true, to_apply=%region_2.3 | all-reduce | flops 2640 | bytes 21120 | tf_op jit(solution)/shard_map/psum | solution.py:121
  32.6 1.3 fusion.63
  34.0 0.4 fusion.47
  34.4 0.8 fusion.38
  35.2 0.6 pad_maximum_fusion.7
  35.9 0.3 copy-done
  36.5 31.5 %all-reduce.3.cloned.1.call-done = (f32[2,2,32,128]{3,2,1,0:T(8,128)}, f32[2,2,32,128]{3,2,1,0:T(8,128)}) async-done(((f32[2,2,32,128]{3,2,1,0:T(8,128)}, f32[2,2,32,128]{3,2,1,0:T(8,128)}), (f32[2,2,32,128]{3,2,1,0:T(8,128)}, f32[2,2,32,128]{3,2,1,0:T(8,128)})) %all-reduce.3.cloned.1.call-update) | async-done | bytes 131088 | tf_op jit(solution)/shard_map/psum | solution.py:123
  67.9 1.1 fusion.69
  69.0 1.5 collective-permute-start
  70.5 0.6 collective-permute-start.1
  71.1 1.0 fusion.70
  72.1 1.5 collective-permute-start.6
  73.5 0.6 collective-permute-start.7
  74.3 1.5 collective-permute-start.10
  75.8 0.6 collective-permute-start.11
  76.4 0.7 collective-permute-done.6
  77.2 1.4 collective-permute-done.7
  79.4 7.7 %collective-permute-done.10 = f32[2,32,12,2]{3,1,2,0:T(8,128)} collective-permute-done((f32[2,32,12,2]{3,1,2,0:T(8,128)S(1)}, f32[2,32,12,2]{3,1,2,0:T(8,128)}, u32[]{:S(2)}, u32[]{:S(2)}) %collective-permute-start.10) | collective-permute-done | bytes 6176 | tf_op jit(solution)/shard_map/ppermute | solution.py:14
  87.1 6.3 %collective-permute-done.11 = f32[2,32,12,2]{3,1,2,0:T(8,128)} collective-permute-done((f32[2,32,12,2]{3,1,2,0:T(8,128)S(1)}, f32[2,32,12,2]{3,1,2,0:T(8,128)}, u32[]{:S(2)}, u32[]{:S(2)}) %collective-permute-start.11) | collective-permute-done | bytes 6176 | tf_op jit(solution)/shard_map/ppermute | solution.py:16
  93.4 1.6 fusion
  95.2 3.4 %psum.38 = f32[12,260]{1,0:T(8,128)S(1)} all-reduce(f32[12,260]{1,0:T(8,128)S(1)} %multiply_reduce_fusion.2), channel_id=1, replica_groups=mesh['groups'=2,'wide'=4,'narrow'=2,'lev'=2] {'lev'}, use_global_device_ids=true, to_apply=%region_5.6 | all-reduce | flops 3120 | bytes 24960 | tf_op jit(solution)/shard_map/psum | solution.py:118
  98.8 0.6 fusion.5
  99.4 0.6 fusion.66
  100.1 0.4 fusion.33
  100.5 0.8 fusion.24
  101.3 1.2 collective-permute-start.12
  102.4 2.7 %collective-permute-start.13 = (f32[2,32,2,256]{3,1,2,0:T(8,128)S(1)}, f32[2,32,2,256]{3,1,2,0:T(8,128)S(1)}, u32[]{:S(2)}, u32[]{:S(2)}) collective-permute-start(f32[2,32,2,256]{3,1,2,0:T(8,128)S(1)} %get-tuple-element.42), channel_id=1, source_target_pairs={{4,0},{8,4},{12,8},{0,12},{5,1},{9,5},{13,9},{1,13},{6,2},{10,6},{... | collective-permute-start | bytes 393224 | tf_op jit(solution)/shard_map/ppermute | solution.py:16
  105.3 4.2 %collective-permute-done.12 = f32[2,32,2,256]{3,1,2,0:T(8,128)S(1)} collective-permute-done((f32[2,32,2,256]{3,1,2,0:T(8,128)S(1)}, f32[2,32,2,256]{3,1,2,0:T(8,128)S(1)}, u32[]{:S(2)}, u32[]{:S(2)}) %collective-permute-start.12) | collective-permute-done | bytes 131104 | tf_op jit(solution)/shard_map/ppermute | solution.py:14
  109.5 1.2 collective-permute-done.13
  111.0 1.5 collective-permute-start.14
  112.5 0.6 collective-permute-start.15
  113.6 9.5 %collective-permute-done.14 = f32[2,32,12,2]{3,1,2,0:T(8,128)S(1)} collective-permute-done((f32[2,32,12,2]{3,1,2,0:T(8,128)S(1)}, f32[2,32,12,2]{3,1,2,0:T(8,128)S(1)}, u32[]{:S(2)}, u32[]{:S(2)}) %collective-permute-start.14) | collective-permute-done | bytes 6176 | tf_op jit(solution)/shard_map/ppermute | solution.py:14
  123.1 6.7 %collective-permute-done.15 = f32[2,32,12,2]{3,1,2,0:T(8,128)} collective-permute-done((f32[2,32,12,2]{3,1,2,0:T(8,128)S(1)}, f32[2,32,12,2]{3,1,2,0:T(8,128)}, u32[]{:S(2)}, u32[]{:S(2)}) %collective-permute-start.15) | collective-permute-done | bytes 6176 | tf_op jit(solution)/shard_map/ppermute | solution.py:16
  129.8 1.5 fusion.1
  131.5 3.6 %psum.39 = f32[12,260]{1,0:T(8,128)S(1)} all-reduce(f32[12,260]{1,0:T(8,128)S(1)} %multiply_reduce_fusion.1), channel_id=1, replica_groups=mesh['groups'=2,'wide'=4,'narrow'=2,'lev'=2] {'lev'}, use_global_device_ids=true, to_apply=%region_7.8 | all-reduce | flops 3120 | bytes 24960 | tf_op jit(solution)/shard_map/psum | solution.py:118
  135.3 0.6 fusion.4
  135.9 0.6 fusion.65
  136.6 0.4 fusion.19
  137.0 0.8 fusion.10
  137.8 5.0 %slice.512 = f32[2,32,4,128]{3,1,2,0:T(8,128)S(1)} slice(f32[2,32,8,256]{3,1,2,0:T(8,128)S(1)} %pad_maximum_fusion.2), slice={[0:2:1], [0:32:1], [0:8:2], [0:256:2]} | slice | bytes 262144 | tf_op jit(solution)/shard_map/slice | solution.py:139
  142.8 5.1 %slice.513 = f32[2,32,4,128]{3,1,2,0:T(8,128)S(1)} slice(f32[2,32,8,256]{3,1,2,0:T(8,128)S(1)} %pad_maximum_fusion.2), slice={[0:2:1], [0:32:1], [1:8:2], [0:256:2]} | slice | bytes 262144 | tf_op jit(solution)/shard_map/slice | solution.py:140
  147.9 5.0 %slice.514 = f32[2,32,4,128]{3,1,2,0:T(8,128)S(1)} slice(f32[2,32,8,256]{3,1,2,0:T(8,128)S(1)} %pad_maximum_fusion.2), slice={[0:2:1], [0:32:1], [0:8:2], [1:256:2]} | slice | bytes 262144 | tf_op jit(solution)/shard_map/slice | solution.py:141
  152.9 5.1 %slice.515 = f32[2,32,4,128]{3,1,2,0:T(8,128)S(1)} slice(f32[2,32,8,256]{3,1,2,0:T(8,128)S(1)} %pad_maximum_fusion.2), slice={[0:2:1], [0:32:1], [1:8:2], [1:256:2]} | slice | bytes 262144 | tf_op jit(solution)/shard_map/slice | solution.py:142
  158.0 1.1 copy.52
  159.1 15.5 %all_gather.3 = f32[2,32,16,128]{3,1,2,0:T(8,128)S(1)} all-gather(f32[2,32,4,128]{3,1,2,0:T(8,128)S(1)} %add_multiply_fusion), channel_id=1, replica_groups=mesh['groups'=2,'wide'=4,'narrow'=2,'lev'=2] {'wide'}, dimensions={2}, use_global_device_ids=true | all-gather | bytes 655360 | tf_op jit(solution)/shard_map/all_gather | solution.py:145
  174.7 0.6 gather_fusion
  175.4 1.1 copy.51
  (78 shorter events, 4.2 us)
Async XLA Ops:
  7.2 12.5 %copy-start.1 = (f32[2,32,16,128]{3,2,1,0:T(8,128)S(1)}, f32[2,32,16,128]{3,2,1,0:T(8,128)}, u32[]{:S(2)}) copy-start(f32[2,32,16,128]{3,2,1,0:T(8,128)} %param.8) | copy-start | bytes 1572868
  7.2 13.2 %copy-start.5 = (f32[32]{0:T(128)S(1)}, f32[32]{0:T(128)}, u32[]{:S(2)}) copy-start(f32[32]{0:T(128)} %param.11) | copy-start | bytes 388
  7.2 13.2 %copy-start.8 = (f32[32]{0:T(128)S(1)}, f32[32]{0:T(128)}, u32[]{:S(2)}) copy-start(f32[32]{0:T(128)} %param.14) | copy-start | bytes 388
  7.2 13.2 %copy-start.7 = (f32[32]{0:T(128)S(1)}, f32[32]{0:T(128)}, u32[]{:S(2)}) copy-start(f32[32]{0:T(128)} %param.12) | copy-start | bytes 388
  7.2 13.2 %copy-start.6 = (f32[32]{0:T(128)S(1)}, f32[32]{0:T(128)}, u32[]{:S(2)}) copy-start(f32[32]{0:T(128)} %param.13) | copy-start | bytes 388
  7.2 60.7 %all-reduce.3.cloned.1.call-start = ((), (), s32[]{:S(2)}) async-start(), calls=%async_computation | async-start | bytes 262144 | tf_op jit(solution)/shard_map/psum | solution.py:123
  8.4 12.1 %collective-permute-start.2 = (f32[2,32,2,128]{3,1,2,0:T(8,128)S(1)}, f32[2,32,2,128]{3,1,2,0:T(8,128)S(1)}, u32[]{:S(2)}, u32[]{:S(2)}) collective-permute-start(f32[2,32,2,128]{3,1,2,0:T(8,128)S(1)} %copy.57), channel_id=1, source_target_pairs={{0,4},{4,8},{8,12},{12,0},{1,5},{5,9},{9,13},{13,1},{2,6},{6,10},{... | collective-permute-start | bytes 196616 | tf_op jit(solution)/shard_map/ppermute | solution.py:14
  11.5 9.2 %collective-permute-start.3 = (f32[2,32,2,128]{3,1,2,0:T(8,128)S(1)}, f32[2,32,2,128]{3,1,2,0:T(8,128)S(1)}, u32[]{:S(2)}, u32[]{:S(2)}) collective-permute-start(f32[2,32,2,128]{3,1,2,0:T(8,128)S(1)} %copy.58), channel_id=1, source_target_pairs={{4,0},{8,4},{12,8},{0,12},{5,1},{9,5},{13,9},{1,13},{6,2},{10,6},{... | collective-permute-start | bytes 196616 | tf_op jit(solution)/shard_map/ppermute | solution.py:16
  15.0 20.9 %collective-permute-start.8 = (f32[2,32,2,256]{3,1,2,0:T(8,128)S(1)}, f32[2,32,2,256]{3,1,2,0:T(8,128)S(1)}, u32[]{:S(2)}, u32[]{:S(2)}) collective-permute-start(f32[2,32,2,256]{3,1,2,0:T(8,128)S(1)} %copy.59), channel_id=1, source_target_pairs={{0,4},{4,8},{8,12},{12,0},{1,5},{5,9},{9,13},{13,1},{2,6},{6,10},{... | collective-permute-start | bytes 393224 | tf_op jit(solution)/shard_map/ppermute | solution.py:14
  15.1 21.3 %collective-permute-start.9 = (f32[2,32,2,256]{3,1,2,0:T(8,128)S(1)}, f32[2,32,2,256]{3,1,2,0:T(8,128)S(1)}, u32[]{:S(2)}, u32[]{:S(2)}) collective-permute-start(f32[2,32,2,256]{3,1,2,0:T(8,128)S(1)} %copy.60), channel_id=1, source_target_pairs={{4,0},{8,4},{12,8},{0,12},{5,1},{9,5},{13,9},{1,13},{6,2},{10,6},{... | collective-permute-start | bytes 393224 | tf_op jit(solution)/shard_map/ppermute | solution.py:16
  21.2 4.1 %collective-permute-start.4 = (f32[2,32,20,2]{1,3,2,0:T(2,128)S(1)}, f32[2,32,20,2]{1,3,2,0:T(2,128)S(1)}, u32[]{:S(2)}, u32[]{:S(2)}) collective-permute-start(f32[2,32,20,2]{1,3,2,0:T(2,128)S(1)} %copy.37), channel_id=1, source_target_pairs={{0,2},{2,0},{1,3},{3,1},{4,6},{6,4},{5,7},{7,5},{8,10},{10,8},{9,1... | collective-permute-start | bytes 30728 | tf_op jit(solution)/shard_map/ppermute | solution.py:14
  23.2 4.1 %collective-permute-start.5 = (f32[2,32,20,2]{1,3,2,0:T(2,128)S(1)}, f32[2,32,20,2]{1,3,2,0:T(2,128)S(1)}, u32[]{:S(2)}, u32[]{:S(2)}) collective-permute-start(f32[2,32,20,2]{1,3,2,0:T(2,128)S(1)} %copy.38), channel_id=1, source_target_pairs={{2,0},{0,2},{3,1},{1,3},{6,4},{4,6},{7,5},{5,7},{10,8},{8,10},{11,... | collective-permute-start | bytes 30728 | tf_op jit(solution)/shard_map/ppermute | solution.py:16
  28.2 0.7 copy-start.4
  35.2 1.1 copy-start
  67.9 10.7 %copy-start.2 = (f32[2,2,32,128]{3,2,1,0:T(8,128)S(1)}, f32[2,2,32,128]{3,2,1,0:T(8,128)}, u32[]{:S(2)}) copy-start(f32[2,2,32,128]{3,2,1,0:T(8,128)} %get-tuple-element.6) | copy-start | bytes 196612
  67.9 10.7 %copy-start.3 = (f32[2,2,32,128]{3,2,1,0:T(8,128)S(1)}, f32[2,2,32,128]{3,2,1,0:T(8,128)}, u32[]{:S(2)}) copy-start(f32[2,2,32,128]{3,2,1,0:T(8,128)} %get-tuple-element.7) | copy-start | bytes 196612
  69.0 6.8 %collective-permute-start = (f32[2,2,32,2]{3,2,1,0:T(8,128)S(1)}, f32[2,2,32,2]{3,2,1,0:T(8,128)S(1)}, u32[]{:S(2)}, u32[]{:S(2)}) collective-permute-start(f32[2,2,32,2]{3,2,1,0:T(8,128)S(1)} %get-tuple-element.51), channel_id=1, source_target_pairs={{0,2},{2,0},{1,3},{3,1},{4,6},{6,4},{5,7},{7,5},{8,10},{10,8},{9,1... | collective-permute-start | bytes 3080 | tf_op jit(solution)/shard_map/ppermute | solution.py:14
  70.5 6.0 %collective-permute-start.1 = (f32[2,2,32,2]{3,2,1,0:T(8,128)S(1)}, f32[2,2,32,2]{3,2,1,0:T(8,128)S(1)}, u32[]{:S(2)}, u32[]{:S(2)}) collective-permute-start(f32[2,2,32,2]{3,2,1,0:T(8,128)S(1)} %get-tuple-element.52), channel_id=1, source_target_pairs={{2,0},{0,2},{3,1},{1,3},{6,4},{4,6},{7,5},{5,7},{10,8},{8,10},{11,... | collective-permute-start | bytes 3080 | tf_op jit(solution)/shard_map/ppermute | solution.py:16
  72.1 5.1 %collective-permute-start.6 = (f32[2,2,32,2]{3,2,1,0:T(8,128)S(1)}, f32[2,2,32,2]{3,2,1,0:T(8,128)S(1)}, u32[]{:S(2)}, u32[]{:S(2)}) collective-permute-start(f32[2,2,32,2]{3,2,1,0:T(8,128)S(1)} %get-tuple-element.53), channel_id=1, source_target_pairs={{0,2},{2,0},{1,3},{3,1},{4,6},{6,4},{5,7},{7,5},{8,10},{10,8},{9,1... | collective-permute-start | bytes 3080 | tf_op jit(solution)/shard_map/ppermute | solution.py:14
  73.5 5.0 %collective-permute-start.7 = (f32[2,2,32,2]{3,2,1,0:T(8,128)S(1)}, f32[2,2,32,2]{3,2,1,0:T(8,128)S(1)}, u32[]{:S(2)}, u32[]{:S(2)}) collective-permute-start(f32[2,2,32,2]{3,2,1,0:T(8,128)S(1)} %get-tuple-element.54), channel_id=1, source_target_pairs={{2,0},{0,2},{3,1},{1,3},{6,4},{4,6},{7,5},{5,7},{10,8},{8,10},{11,... | collective-permute-start | bytes 3080 | tf_op jit(solution)/shard_map/ppermute | solution.py:16
  74.3 12.8 %collective-permute-start.10 = (f32[2,32,12,2]{3,1,2,0:T(8,128)S(1)}, f32[2,32,12,2]{3,1,2,0:T(8,128)}, u32[]{:S(2)}, u32[]{:S(2)}) collective-permute-start(f32[2,32,12,2]{3,1,2,0:T(8,128)S(1)} %get-tuple-element.18), channel_id=1, source_target_pairs={{0,2},{2,0},{1,3},{3,1},{4,6},{6,4},{5,7},{7,5},{8,10},{10,8},{9,1... | collective-permute-start | bytes 18440 | tf_op jit(solution)/shard_map/ppermute | solution.py:14
  75.8 17.5 %collective-permute-start.11 = (f32[2,32,12,2]{3,1,2,0:T(8,128)S(1)}, f32[2,32,12,2]{3,1,2,0:T(8,128)}, u32[]{:S(2)}, u32[]{:S(2)}) collective-permute-start(f32[2,32,12,2]{3,1,2,0:T(8,128)S(1)} %get-tuple-element.19), channel_id=1, source_target_pairs={{2,0},{0,2},{3,1},{1,3},{6,4},{4,6},{7,5},{5,7},{10,8},{8,10},{11,... | collective-permute-start | bytes 18440 | tf_op jit(solution)/shard_map/ppermute | solution.py:16
  101.3 8.2 %collective-permute-start.12 = (f32[2,32,2,256]{3,1,2,0:T(8,128)S(1)}, f32[2,32,2,256]{3,1,2,0:T(8,128)S(1)}, u32[]{:S(2)}, u32[]{:S(2)}) collective-permute-start(f32[2,32,2,256]{3,1,2,0:T(8,128)S(1)} %get-tuple-element.41), channel_id=1, source_target_pairs={{0,4},{4,8},{8,12},{12,0},{1,5},{5,9},{9,13},{13,1},{2,6},{6,10},{... | collective-permute-start | bytes 393224 | tf_op jit(solution)/shard_map/ppermute | solution.py:14
  102.4 8.3 %collective-permute-start.13 = (f32[2,32,2,256]{3,1,2,0:T(8,128)S(1)}, f32[2,32,2,256]{3,1,2,0:T(8,128)S(1)}, u32[]{:S(2)}, u32[]{:S(2)}) collective-permute-start(f32[2,32,2,256]{3,1,2,0:T(8,128)S(1)} %get-tuple-element.42), channel_id=1, source_target_pairs={{4,0},{8,4},{12,8},{0,12},{5,1},{9,5},{13,9},{1,13},{6,2},{10,6},{... | collective-permute-start | bytes 393224 | tf_op jit(solution)/shard_map/ppermute | solution.py:16
  111.0 12.1 %collective-permute-start.14 = (f32[2,32,12,2]{3,1,2,0:T(8,128)S(1)}, f32[2,32,12,2]{3,1,2,0:T(8,128)S(1)}, u32[]{:S(2)}, u32[]{:S(2)}) collective-permute-start(f32[2,32,12,2]{3,1,2,0:T(8,128)S(1)} %get-tuple-element.16), channel_id=1, source_target_pairs={{0,2},{2,0},{1,3},{3,1},{4,6},{6,4},{5,7},{7,5},{8,10},{10,8},{9,1... | collective-permute-start | bytes 18440 | tf_op jit(solution)/shard_map/ppermute | solution.py:14
  112.5 17.3 %collective-permute-start.15 = (f32[2,32,12,2]{3,1,2,0:T(8,128)S(1)}, f32[2,32,12,2]{3,1,2,0:T(8,128)}, u32[]{:S(2)}, u32[]{:S(2)}) collective-permute-start(f32[2,32,12,2]{3,1,2,0:T(8,128)S(1)} %get-tuple-element.17), channel_id=1, source_target_pairs={{2,0},{0,2},{3,1},{1,3},{6,4},{4,6},{7,5},{5,7},{10,8},{8,10},{11,... | collective-permute-start | bytes 18440 | tf_op jit(solution)/shard_map/ppermute | solution.py:16
Sparse Core Ops, SparseCore 0:
  36.0 31.8 all-reduce.2
where the time goes:
time: 184 us; the launch traced here: 183 us
  waiting for transfers between devices  72.5 us (39%)
  local copies, waits for them, and re-layouts  33.7 us (18%)
  blocking collectives  25.9 us (14%)
  starting transfers between devices  23.5 us (13%)
  between operations  15.3 us (8%)
  other arithmetic  12.5 us (7%)
    psum x1, waiting for transfers between devices, shards(): lax.psum((cycle_rows(parent_state, anchor, band_rows, position), cycle_ro...  31.5 us
    ppermute x8, waiting for transfers between devices, padded(): lax.ppermute(tail, axis, [(i, (i + 1) % count) for i in range(count)])  23.7 us
    ppermute x8, waiting for transfers between devices, padded(): lax.ppermute(head, axis, [((i + 1) % count, i) for i in range(count)])  17.2 us
    all_gather x1, blocking collectives, shards(): lax.all_gather(coarse, 'wide', axis=2, tiled=True)  15.5 us
    ppermute x8, starting transfers between devices, padded(): lax.ppermute(tail, axis, [(i, (i + 1) % count) for i in range(count)])  12 us
    ppermute x8, starting transfers between devices, padded(): lax.ppermute(head, axis, [((i + 1) % count, i) for i in range(count)])  11.5 us
    psum x2, blocking collectives, nest_step(): nest_column = lax.psum(column_part(extended, level_weights), 'lev')  7.02 us
    slice x1, local copies, waits for them, and re-layouts, shards(): nest_out[:, :, 1::2, 0::2]  5.11 us
  transfers between devices with their start and end apart: 17, of which 11 were waited for; matrix products, arithmetic and copies ran while one was open for 6% of the time, Pallas kernels for 0%

commit v1 on v0

v1 whole, which is shorter than its diff:
```python
import functools
import jax
import jax.numpy as jnp
from jax import lax
from jax.experimental import pallas as pl
from jax.experimental.pallas import tpu as pltpu
from jax.sharding import PartitionSpec as P

T = 128


def roll(x, shift):
    return pltpu.roll(x, shift, axis=1)


def kernel(
    W, N, anchor_ref, cf_ref, p_ref, n_ref, po_ref, no_ref,
    pe, ne, ne2, lp, ln, cb, pack, pack2, cr, cr2,
    psp, prp, psn, prn, psm, prm, pick, tips, slots0, slots1, corners0, corners1, cg, ssem, rsem,
):
    R, K, C = p_ref.shape[1:]
    r, c = n_ref.shape[1], n_ref.shape[3]
    half = r // 2
    slots, corners = (slots0, slots1), (corners0, corners1)
    band = half * W
    w, n, lev = lax.axis_index("wide"), lax.axis_index("narrow"), lax.axis_index("lev")
    anchor = anchor_ref[0]
    steps = (1,) if N == 2 else (1, N - 1)
    other = {"lev": 1 - lev}
    lane = lax.broadcasted_iota(jnp.int32, (K, T), 1)

    barrier = pltpu.get_barrier_semaphore()
    count = 0
    for dw in range(W):
        for dn in (0,) + steps:
            if dw or dn:
                pl.semaphore_signal(
                    barrier, inc=1, device_id_type=pl.DeviceIdType.MESH,
                    device_id={"wide": lax.rem(w + dw, W), "narrow": lax.rem(n + dn, N)},
                )
                count += 1
    pl.semaphore_signal(barrier, inc=1, device_id=other, device_id_type=pl.DeviceIdType.MESH)

    next_send, next_recv, pending = [0], [0], []

    def take(many=1):
        next_recv[0] += many
        return next_recv[0] - many

    def guarded(cond, act):
        if cond is None:
            act()
        else:
            pl.when(cond)(act)

    def send(src, dst, sem, device, cond=None):
        copy = pltpu.make_async_remote_copy(
            src_ref=src, dst_ref=dst, send_sem=ssem.at[next_send[0]], recv_sem=rsem.at[sem],
            device_id=device, device_id_type=pl.DeviceIdType.MESH,
        )
        next_send[0] += 1
        guarded(cond, lambda: copy.start())
        pending.append((copy, cond))

    def receive(dst, sem, cond=None):
        copy = pltpu.make_async_remote_copy(
            src_ref=dst, dst_ref=dst, send_sem=ssem.at[0], recv_sem=rsem.at[sem],
            device_id=other, device_id_type=pl.DeviceIdType.MESH,
        )
        guarded(cond, lambda: copy.wait_recv())

    above, below = w > 0, w < W - 1
    up, down = {"wide": w - 1}, {"wide": w + 1}
    waits = []

    def send_rows(src, start, dst, rows, lanes):
        s = take(4)
        at = lambda ref, f, i, m: ref.at[f, pl.ds(i, m), :, pl.ds(0, lanes)]
        for f, m, k in ((0, 2, 0), (1, 1, 1)):
            send(at(src, f, start + rows - m, m), at(dst, f, 2 - m, m), s + k, down, below)
            send(at(src, f, start, m), at(dst, f, rows + 2, m), s + 2 + k, up, above)

        def wait():
            for f, m, k in ((0, 2, 0), (1, 1, 1)):
                receive(at(dst, f, 2 - m, m), s + k, above)
                receive(at(dst, f, rows + 2, m), s + 2 + k, below)
        return wait

    def send_packs(src, dst, first):
        todo = []
        for d, dn in enumerate(steps):
            to = lax.rem(n + dn, N)
            s = take(3)
            send(src, dst.at[d, 1], s + 1, {"narrow": to})
            tip = src.at[pl.ds(first, 1)]
            send(tip, dst.at[d, 0, pl.ds(first, 1)], s, {"wide": w + 1, "narrow": to}, below)
            send(tip, dst.at[d, 2, pl.ds(first, 1)], s + 2, {"wide": w - 1, "narrow": to}, above)
            todo.append((dst.at[d, 1], s + 1, None))
            todo.append((dst.at[d, 0, pl.ds(first, 1)], s, above))
            todo.append((dst.at[d, 2, pl.ds(first, 1)], s + 2, below))
        return lambda: [receive(*one) for one in todo]

    def merged(dst, at, tile, even):
        if N == 2:
            return dst[0, at, tile]
        return jnp.where(even, dst[0, at, tile], dst[1, at, tile])

    def ends(value, lanes):
        return jnp.where(lane < T // 2, value[:, :T], value[:, lanes - T:lanes])

    def send_picks(source, k):
        s = take(W)
        sems = [take(W) for _ in steps]
        for e, (row, target, cond) in enumerate((
            (anchor - 1, 0, w != 0), (anchor + band, W - 1, w != W - 1),
        )):
            local = jnp.clip(row - w * R, 0, R - 1)
            for f in range(2):
                pick[k, e, f] = source[f, local]
            tips[k, e] = ends(pick[k, e, 0], C)
            send(pick.at[k, e], slots[k].at[w], s + w, {"wide": target}, cond)
            for d, dn in enumerate(steps):
                send(
                    tips.at[k, e], corners[k].at[d, w], sems[d] + w,
                    {"wide": target, "narrow": lax.rem(n + dn, N)}, cond,
                )
        for e, target in ((0, 0), (1, W - 1)):
            for d, dn in enumerate(steps):
                send(
                    tips.at[k, e], corners[k].at[d, w], sems[d] + w,
                    {"narrow": lax.rem(n + dn, N)}, w == target,
                )

            def keep(e=e):
                slots[k][w] = pick[k, e]
            pl.when(w == target)(keep)

        def wait():
            for target in (0, W - 1):
                for src in range(W):
                    if src != target:
                        receive(slots[k].at[src], s + src, w == target)
                    for d in range(len(steps)):
                        receive(corners[k].at[d, src], sems[d] + src, w == target)
        return wait

    def set_edges(dst, ks):
        scale = 1.0 / len(ks)
        wider = (
            lax.broadcasted_iota(jnp.int32, (C, c), 1) // 2
            == lax.broadcasted_iota(jnp.int32, (C, c), 0)
        ).astype(jnp.float32)
        for row, target, first, near in (
            (anchor - 1, 0, 0, 1), (anchor + band, W - 1, r + 2, r + 2),
        ):
            owner = lax.div(row, R)

            def fill(owner=owner, first=first, near=near):
                for f in range(2):
                    value = scale * sum(slots[k][owner, f] for k in ks)
                    fine = jnp.dot(
                        value, wider, precision=lax.Precision.HIGHEST,
                        preferred_element_type=jnp.float32,
                    )
                    dst[f, first, :, 0:c] = fine
                    dst[f, first + 1, :, 0:c] = fine
                left = scale * sum(corners[k][0, owner] for k in ks)
                if N > 2:
                    right = scale * sum(corners[k][1, owner] for k in ks)
                    left = jnp.where(lane < T // 2, right, left)
                dst[0, near, :, c:c + T] = left
            pl.when(w == target)(fill)

    def column_sums(ext, rows, out):
        weights = cb[0, :, 0:ext.shape[3]]

        def body(j, _):
            out[pl.ds(j, 1), :] = jnp.sum(weights * ext[0, j + 1], axis=0, keepdims=True)
            return 0
        lax.fori_loop(0, rows + 2, body, 0)

    def advance(ext, rows, lanes, mine, theirs, lap, f, g, store):
        L = lanes + T
        near = lambda x: roll(x, 1) + roll(x, L - 1)

        def inner(j, _):
            x = ext[0, j + 1]
            lap[j] = ext[0, j + 2] + ext[0, j] + near(x) - 4.0 * x
            return 0
        lax.fori_loop(0, rows + 2, inner, 0)
        diffuse, smooth = f * cb[1, :, 0:lanes], g * cb[2, :, 0:lanes]
        couple, advect = f * cb[3, :, 0:lanes], f * cb[4, :, 0:lanes]

        def body(i, _):
            total = lambda j: mine[pl.ds(j, 1), :] + theirs[pl.ds(j, 1), :]
            p0, p1, p2 = total(i), total(i + 1), total(i + 2)
            wide1 = jnp.broadcast_to(p1, (8, L))
            pl_, pr = roll(wide1, 1)[0:1, :lanes], roll(wide1, L - 1)[0:1, :lanes]
            p0, p1, p2 = p0[:, :lanes], p1[:, :lanes], p2[:, :lanes]
            lap_p = p2 + p0 + pr + pl_ - 4.0 * p1
            drp, dcp = 0.5 * (p2 - p0), 0.5 * (pr - pl_)
            l1 = lap[i + 1]
            m1 = l1[:, :lanes]
            lap2 = lap[i + 2][:, :lanes] + lap[i][:, :lanes] + near(l1)[:, :lanes] - 4.0 * m1
            h = ext[0, i + 2][:, :lanes]
            store(0, i, h + diffuse * m1 - smooth * lap2 + couple * lap_p)
            q = ext[1, i + 2]
            qu, qd, q1 = ext[1, i + 1][:, :lanes], ext[1, i + 3][:, :lanes], q[:, :lanes]
            ql, qr = roll(q, 1)[:, :lanes], roll(q, L - 1)[:, :lanes]
            lap_q = qd + qu + qr + ql - 4.0 * q1
            drift = drp * (0.5 * (qd - qu)) + dcp * (0.5 * (qr - ql))
            store(1, i, q1 + diffuse * lap_q - advect * drift)
            return 0
        lax.fori_loop(0, rows, body, 0)

    def pack_nest(ref, start, dst, tile):
        dst[tile] = jnp.zeros((K, T), jnp.float32)

        def body(i, _):
            for f in range(2):
                slot = f * r + i
                x = ends(ref[f, i + start], c)
                dst[tile] = jnp.where(lane // 4 == slot, roll(x, 4 * slot + 2), dst[tile])
            return 0
        lax.fori_loop(0, r, body, 0)

    pl.semaphore_wait(barrier, count + 1)
    wait_rows = [send_rows(p_ref, 0, pe, R, C), send_rows(n_ref, 0, ne, r, c)]
    wait_old = send_picks(p_ref, 0)
    pack[0] = jnp.zeros((K, T), jnp.float32)

    def pack_parent(i, _):
        for f in range(2):
            slot = f * R + i
            x = ends(p_ref[f, i], C)
            pack[0] = jnp.where(lane // 4 == slot, roll(x, 4 * slot + 2), pack[0])
        return 0
    lax.fori_loop(0, R, pack_parent, 0)
    pack_nest(n_ref, 0, pack, 1)
    for slot, row in ((2 * r, 0), (2 * r + 1, R - 1)):
        x = ends(p_ref[0, row], C)
        pack[1] = jnp.where(lane // 4 == slot, roll(x, 4 * slot + 2), pack[1])
    wait_packs = send_packs(pack, cr, 1)

    for j in range(5):
        cb[j] = jnp.broadcast_to(cf_ref[:, j:j + 1], cb.shape[1:])
    for f in range(2):
        pe[f, 2:R + 2, :, 0:C] = p_ref[f]
        ne[f, 2:r + 2, :, 0:c] = n_ref[f]
    for cond, first in ((w == 0, 0), (w == W - 1, R + 2)):
        def clear(first=first):
            pe[:, first:first + 2] = jnp.zeros((2, 2, K, C + T), jnp.float32)
        pl.when(cond)(clear)
    left_part = lane % 4 < 2
    side = lambda slot: lax.rem(2 * T - 2 - 4 * slot, T)
    wait_packs()
    m0 = merged(cr, 1, 0, left_part)
    m1 = merged(cr, 1, 1, left_part)

    def unpack_parent(i, _):
        for f in range(2):
            pe[f, i + 2, :, C:C + T] = roll(m0, side(f * R + i))
        return 0
    lax.fori_loop(0, R, unpack_parent, 0)

    def unpack_nest(dst, m):
        def body(i, _):
            for f in range(2):
                dst[f, i + 2, :, c:c + T] = roll(m, side(f * r + i))
            return 0
        lax.fori_loop(0, r, body, 0)
    unpack_nest(ne, m1)

    @pl.when(above)
    def _():
        m = merged(cr, 0, 1, left_part)
        pe[0, 1, :, C:C + T] = roll(m, side(2 * r + 1))
        ne[0, 1, :, c:c + T] = roll(m, side(r - 1))

    @pl.when(below)
    def _():
        m = merged(cr, 2, 1, left_part)
        pe[0, R + 2, :, C:C + T] = roll(m, side(2 * r))
        ne[0, r + 2, :, c:c + T] = roll(m, side(0))

    def share(mine, theirs):
        s = take()
        send(mine, theirs, s, other)
        return lambda: receive(theirs, s)

    wait_rows[0]()
    column_sums(pe, R, psp)
    wait_p = share(psp, prp)
    wait_rows[1]()
    wait_old()
    set_edges(ne, (0,))
    column_sums(ne, r, psn)
    wait_n = share(psn, prn)
    wait_p()

    def store_parent(f, i, v):
        po_ref[f, i] = v

    def store_mid(f, i, v):
        ne2[f, i + 2, :, 0:c] = v

    def store_nest(f, i, v):
        no_ref[f, i] = v

    advance(pe, R, C, psp, prp, lp, 1.0, 1.0, store_parent)
    wait_new = send_picks(po_ref, 1)
    wait_n()
    advance(ne, r, c, psn, prn, ln, 2.0, 8.0, store_mid)
    wait_mid = send_rows(ne2, 2, ne2, r, c)
    pack_nest(ne2, 2, pack2, 0)
    wait_packs2 = send_packs(pack2, cr2, 0)
    wait_new()
    set_edges(ne2, (0, 1))
    wait_packs2()
    unpack_nest(ne2, merged(cr2, 1, 0, left_part))

    @pl.when(above)
    def _():
        ne2[0, 1, :, c:c + T] = roll(merged(cr2, 0, 0, left_part), side(r - 1))

    @pl.when(below)
    def _():
        ne2[0, r + 2, :, c:c + T] = roll(merged(cr2, 2, 0, left_part), side(0))

    wait_mid()
    column_sums(ne2, r, psm)
    wait_m = share(psm, prm)
    wait_m()
    advance(ne2, r, c, psm, prm, ln, 2.0, 8.0, store_nest)
    narrower = jnp.where(
        lax.broadcasted_iota(jnp.int32, (c, C), 0) // 2
        == lax.broadcasted_iota(jnp.int32, (c, C), 1), 0.25, 0.0
    )
    base = w * half
    for i in range(half):
        for f in range(2):
            cg[base + i, f] = jnp.dot(
                no_ref[f, 2 * i] + no_ref[f, 2 * i + 1], narrower,
                precision=lax.Precision.HIGHEST, preferred_element_type=jnp.float32,
            )
    s = take(W)
    for dw in range(1, W):
        block = cg.at[pl.ds(base, half)]
        send(block, block, s + w, {"wide": lax.rem(w + dw, W)})
    for dw in range(1, W):
        src = lax.rem(w + dw, W)
        receive(cg.at[pl.ds(src * half, half)], s + src)

    def absorb(i, _):
        at = w * R + i - anchor
        inside = (at >= 0) & (at < band)
        piece = jnp.clip(at, 0, band - 1)
        for f in range(2):
            po_ref[f, i] = jnp.where(inside, cg[piece, f], po_ref[f, i])
        return 0
    lax.fori_loop(0, R, absorb, 0)
    for copy, cond in pending:
        guarded(cond, lambda copy=copy: copy.wait_send())


def shards(
    W, N, parent_state, nest_state, level_weights, diffusion, smoothing, coupling, transport, nest_anchor
):
    p = jnp.swapaxes(parent_state, 1, 2)
    q = jnp.swapaxes(nest_state, 1, 2)
    cf = jnp.stack([level_weights, diffusion, smoothing, coupling, transport], axis=1)
    _, R, K, C = p.shape
    r, c = q.shape[1], q.shape[3]
    D = 1 if N == 2 else 2
    F = lambda *dims: pltpu.VMEM(dims, jnp.float32)
    up8 = lambda x: -(-x // 8) * 8
    sums = lambda rows, lanes: F(up8(rows + 2), lanes + T)
    nsem = 40 + 16 * D + 4 * W * (1 + D)
    vm = pl.BlockSpec(memory_space=pltpu.VMEM)
    a, b = pl.pallas_call(
        functools.partial(kernel, W, N),
        out_shape=(
            jax.ShapeDtypeStruct(p.shape, jnp.float32), jax.ShapeDtypeStruct(q.shape, jnp.float32),
        ),
        in_specs=[pl.BlockSpec(memory_space=pltpu.SMEM), vm, vm, vm],
        out_specs=(vm, vm),
        scratch_shapes=[
            F(2, R + 4, K, C + T), F(2, r + 4, K, c + T), F(2, r + 4, K, c + T),
            F(R + 2, K, C + T), F(r + 2, K, c + T), F(5, K, max(C, c) + T),
            F(2, K, T), F(1, K, T), F(D, 3, 2, K, T), F(D, 3, 1, K, T),
            sums(R, C), sums(R, C), sums(r, c), sums(r, c), sums(r, c), sums(r, c),
            F(2, 2, 2, K, C), F(2, 2, K, T), F(W, 2, K, C), F(W, 2, K, C), F(D, W, K, T), F(D, W, K, T),
            F(W * (r // 2), 2, K, C),
            pltpu.SemaphoreType.DMA((nsem,)), pltpu.SemaphoreType.DMA((nsem,)),
        ],
        compiler_params=pltpu.CompilerParams(
            collective_id=0, has_side_effects=True, vmem_limit_bytes=48 * 1024 * 1024,
        ),
    )(nest_anchor, cf, p, q)
    return jnp.swapaxes(a, 1, 2), jnp.swapaxes(b, 1, 2)


def solution(mesh):
    state = P(None, "lev", ("groups", "wide"), "narrow")
    return jax.shard_map(
        functools.partial(shards, mesh.shape["wide"], mesh.shape["narrow"]),
        mesh=mesh,
        in_specs=(state, state) + (P("lev"),) * 5 + (P("groups"),),
        out_specs=(state, state),
        check_vma=False,
    )
```

time: 184 us -> 51.2 us (0.28)
  waiting for transfers between devices: 72.5 us -> 0 us
  Pallas kernels: 0 us -> 44.9 us
  local copies, waits for them, and re-layouts: 33.7 us -> 4.41 us
  blocking collectives: 25.9 us -> 0 us
  starting transfers between devices: 23.5 us -> 0 us
  between operations: 15.3 us -> 1.35 us
  other arithmetic: 12.5 us -> 0 us
    pallas_call x0 -> x1, Pallas kernels: none -> 44.9 us  [shards(): pl.pallas_call(functools.partial(kernel, W, N), out_shape=(jax.ShapeDtype...]
    ppermute x16 -> x0, waiting for transfers between devices: 41 us -> none  [the longest x8 23.7 us: padded(): lax.ppermute(tail, axis, [(i, (i + 1) % count) for i in range(count)])]
    psum x1 -> x0, waiting for transfers between devices: 31.5 us -> none  [shards(): lax.psum((cycle_rows(parent_state, anchor, band_rows, position), cycle_ro...]
    slice x18 -> x0, local copies, waits for them, and re-layouts: 27.4 us -> none  [the longest x1 5.11 us: shards(): nest_out[:, :, 1::2, 0::2]]
    ppermute x16 -> x0, starting transfers between devices: 23.5 us -> none  [the longest x8 12 us: padded(): lax.ppermute(tail, axis, [(i, (i + 1) % count) for i in range(count)])]
    all_gather x1 -> x0, blocking collectives: 15.5 us -> none  [shards(): lax.all_gather(coarse, 'wide', axis=2, tiled=True)]
    psum x3 -> x0, blocking collectives: 10.4 us -> none  [the longest x2 7.02 us: nest_step(): nest_column = lax.psum(column_part(extended, level_weights), 'lev')]
    another operation x9 -> x0, other arithmetic: 4.86 us -> none  [the longest x7 3.59 us: advance(): return jnp.stack([new_height, new_tracer])]
  transfers between devices with their start and end apart: 17 -> 0, of which waited for: 11 -> 0; matrix products, arithmetic and copies ran while one was open for 6% -> 0% of each run, Pallas kernels for 0% -> 0%
where the time goes in v1:
time: 51.2 us; the launch traced here: 50.6 us
  Pallas kernels  44.9 us (88%)
  local copies, waits for them, and re-layouts  4.41 us (9%)
  between operations  1.35 us (3%)
    pallas_call x1, Pallas kernels, shards(): pl.pallas_call(functools.partial(kernel, W, N), out_shape=(jax.ShapeDtype...  44.9 us
    unnamed x16, local copies, waits for them, and re-layouts  4.3 us

profile of v1, /device:TPU:0, one launch (start us, length us, event | category | flops | bytes accessed | tf_op | source)
XLA Modules:
  0.0 50.6 jit_solution(3816445530616230134)
XLA Ops:
  1.3 0.0 copy-start.4
  1.3 0.0 copy-start.5
  1.3 0.0 copy-start.1
  1.3 0.0 copy-start.2
  1.3 0.0 copy-start.3
  1.3 0.6 %copy-done.4 = f32[32]{0:T(128)S(1)} copy-done((f32[32]{0:T(128)S(1)}, f32[32]{0:T(128)}, u32[]{:S(2)}) %copy-start.4) | copy-done | bytes 152
  1.9 0.0 copy-done.5
  2.0 0.0 copy-done.1
  2.0 0.0 copy-done.2
  2.0 0.0 copy-done.3
  2.0 0.1 copy.21.cf_ref
  2.1 0.0 copy-start
  2.1 1.3 %copy.27 = f32[2,32,16,128]{3,1,2,0:T(8,128)S(1)} copy(f32[2,32,16,128]{3,2,1,0:T(8,128)} %param.8) | data formatting | bytes 1048576 | tf_op args[0]
  3.4 0.0 copy-done
  3.4 0.2 copy.26
  3.6 44.9 %shard_map.95 = (f32[2,16,32,128]{3,2,1,0:T(8,128)S(1)}, f32[2,8,32,256]{3,2,1,0:T(8,128)S(1)}) custom-call(s32[1]{0:T(128)S(6)} %copy.28.anchor_ref, f32[32,5]{1,0:T(8,128)S(1)} %copy.21.cf_ref, f32[2,16,32,128]{3,2,1,0:T(8,128)S(1)} %bitcast.13, f32[2,8,32,256]{3,2,1,0:T(8,128)S(1)} %bitcast.14), custom_call_target="tpu_custom_call" | custom-call | tf_op jit(solution)/shard_map/pallas_call | solution.py:380
  48.4 1.1 %copy.22 = f32[2,32,16,128]{3,2,1,0:T(8,128)} copy(f32[2,32,16,128]{3,1,2,0:T(8,128)S(1)} %bitcast.16) | data formatting | bytes 1048576
  49.5 1.1 %copy.23 = f32[2,32,8,256]{3,2,1,0:T(8,128)} copy(f32[2,32,8,256]{3,1,2,0:T(8,128)S(1)} %bitcast.15) | data formatting | bytes 1048576
  (1 shorter events, 0.0 us)
Async XLA Ops:
  1.3 0.7 %copy-start.4 = (f32[32]{0:T(128)S(1)}, f32[32]{0:T(128)}, u32[]{:S(2)}) copy-start(f32[32]{0:T(128)} %param.13) | copy-start | bytes 388
  1.3 0.7 %copy-start.5 = (f32[32]{0:T(128)S(1)}, f32[32]{0:T(128)}, u32[]{:S(2)}) copy-start(f32[32]{0:T(128)} %param.14) | copy-start | bytes 388
  1.3 0.7 %copy-start.1 = (f32[32]{0:T(128)S(1)}, f32[32]{0:T(128)}, u32[]{:S(2)}) copy-start(f32[32]{0:T(128)} %param.10) | copy-start | bytes 388
  1.3 0.7 %copy-start.2 = (f32[32]{0:T(128)S(1)}, f32[32]{0:T(128)}, u32[]{:S(2)}) copy-start(f32[32]{0:T(128)} %param.11) | copy-start | bytes 388
  1.3 0.7 %copy-start.3 = (f32[32]{0:T(128)S(1)}, f32[32]{0:T(128)}, u32[]{:S(2)}) copy-start(f32[32]{0:T(128)} %param.12) | copy-start | bytes 388
  2.1 1.3 %copy-start = (f32[2,32,8,256]{3,2,1,0:T(8,128)S(1)}, f32[2,32,8,256]{3,2,1,0:T(8,128)}, u32[]{:S(2)}) copy-start(f32[2,32,8,256]{3,2,1,0:T(8,128)} %param.9) | copy-start | bytes 1572868

commit v2 on v1

--- a/solution.py
+++ b/solution.py
@@ -177,7 +177,7 @@
         def body(j, _):
             out[pl.ds(j, 1), :] = jnp.sum(weights * ext[0, j + 1], axis=0, keepdims=True)
             return 0
-        lax.fori_loop(0, rows + 2, body, 0)
+        lax.fori_loop(0, rows + 2, body, 0, unroll=True)
 
     def advance(ext, rows, lanes, mine, theirs, lap, f, g, store):
         L = lanes + T
@@ -187,7 +187,7 @@
             x = ext[0, j + 1]
             lap[j] = ext[0, j + 2] + ext[0, j] + near(x) - 4.0 * x
             return 0
-        lax.fori_loop(0, rows + 2, inner, 0)
+        lax.fori_loop(0, rows + 2, inner, 0, unroll=True)
         diffuse, smooth = f * cb[1, :, 0:lanes], g * cb[2, :, 0:lanes]
         couple, advect = f * cb[3, :, 0:lanes], f * cb[4, :, 0:lanes]
 
@@ -211,7 +211,7 @@
             drift = drp * (0.5 * (qd - qu)) + dcp * (0.5 * (qr - ql))
             store(1, i, q1 + diffuse * lap_q - advect * drift)
             return 0
-        lax.fori_loop(0, rows, body, 0)
+        lax.fori_loop(0, rows, body, 0, unroll=True)
 
     def pack_nest(ref, start, dst, tile):
         dst[tile] = jnp.zeros((K, T), jnp.float32)
@@ -222,7 +222,7 @@
                 x = ends(ref[f, i + start], c)
                 dst[tile] = jnp.where(lane // 4 == slot, roll(x, 4 * slot + 2), dst[tile])
             return 0
-        lax.fori_loop(0, r, body, 0)
+        lax.fori_loop(0, r, body, 0, unroll=True)
 
     pl.semaphore_wait(barrier, count + 1)
     wait_rows = [send_rows(p_ref, 0, pe, R, C), send_rows(n_ref, 0, ne, r, c)]
@@ -235,7 +235,7 @@
             x = ends(p_ref[f, i], C)
             pack[0] = jnp.where(lane // 4 == slot, roll(x, 4 * slot + 2), pack[0])
         return 0
-    lax.fori_loop(0, R, pack_parent, 0)
+    lax.fori_loop(0, R, pack_parent, 0, unroll=True)
     pack_nest(n_ref, 0, pack, 1)
     for slot, row in ((2 * r, 0), (2 * r + 1, R - 1)):
         x = ends(p_ref[0, row], C)
@@ -261,14 +261,14 @@
         for f in range(2):
             pe[f, i + 2, :, C:C + T] = roll(m0, side(f * R + i))
         return 0
-    lax.fori_loop(0, R, unpack_parent, 0)
+    lax.fori_loop(0, R, unpack_parent, 0, unroll=True)
 
     def unpack_nest(dst, m):
         def body(i, _):
             for f in range(2):
                 dst[f, i + 2, :, c:c + T] = roll(m, side(f * r + i))
             return 0
-        lax.fori_loop(0, r, body, 0)
+        lax.fori_loop(0, r, body, 0, unroll=True)
     unpack_nest(ne, m1)
 
     @pl.when(above)
@@ -358,7 +358,7 @@
         for f in range(2):
             po_ref[f, i] = jnp.where(inside, cg[piece, f], po_ref[f, i])
         return 0
-    lax.fori_loop(0, R, absorb, 0)
+    lax.fori_loop(0, R, absorb, 0, unroll=True)
     for copy, cond in pending:
         guarded(cond, lambda copy=copy: copy.wait_send())
 

time: 51.2 us -> 43.2 us (0.84)
  Pallas kernels: 44.9 us -> 37 us
    pallas_call x1, Pallas kernels: 44.9 us -> 37 us  [shards(): pl.pallas_call(functools.partial(kernel, W, N), out_shape=(jax.ShapeDtype...]
where the time goes in v2:
time: 43.2 us; the launch traced here: 42.7 us
  Pallas kernels  37 us (86%)
  local copies, waits for them, and re-layouts  4.41 us (10%)
  between operations  1.35 us (3%)
    pallas_call x1, Pallas kernels, shards(): pl.pallas_call(functools.partial(kernel, W, N), out_shape=(jax.ShapeDtype...  37 us
    unnamed x16, local copies, waits for them, and re-layouts  4.3 us

profile of v2, /device:TPU:0, one launch (start us, length us, event | category | flops | bytes accessed | tf_op | source)
XLA Modules:
  0.0 42.7 jit_solution(717952777640619511)
XLA Ops:
  1.3 0.0 copy-start.4
  1.3 0.0 copy-start.5
  1.3 0.0 copy-start.1
  1.3 0.0 copy-start.2
  1.3 0.0 copy-start.3
  1.3 0.6 %copy-done.4 = f32[32]{0:T(128)S(1)} copy-done((f32[32]{0:T(128)S(1)}, f32[32]{0:T(128)}, u32[]{:S(2)}) %copy-start.4) | copy-done | bytes 152
  1.9 0.0 copy-done.5
  2.0 0.0 copy-done.1
  2.0 0.0 copy-done.2
  2.0 0.0 copy-done.3
  2.0 0.1 copy.21.cf_ref
  2.1 0.0 copy-start
  2.1 1.3 %copy.27 = f32[2,32,16,128]{3,1,2,0:T(8,128)S(1)} copy(f32[2,32,16,128]{3,2,1,0:T(8,128)} %param.8) | data formatting | bytes 1048576 | tf_op args[0]
  3.4 0.0 copy-done
  3.4 0.2 copy.26
  3.6 37.0 %shard_map.95 = (f32[2,16,32,128]{3,2,1,0:T(8,128)S(1)}, f32[2,8,32,256]{3,2,1,0:T(8,128)S(1)}) custom-call(s32[1]{0:T(128)S(6)} %copy.28.anchor_ref, f32[32,5]{1,0:T(8,128)S(1)} %copy.21.cf_ref, f32[2,16,32,128]{3,2,1,0:T(8,128)S(1)} %bitcast.13, f32[2,8,32,256]{3,2,1,0:T(8,128)S(1)} %bitcast.14), custom_call_target="tpu_custom_call" | custom-call | tf_op jit(solution)/shard_map/pallas_call | solution.py:380
  40.5 1.1 %copy.22 = f32[2,32,16,128]{3,2,1,0:T(8,128)} copy(f32[2,32,16,128]{3,1,2,0:T(8,128)S(1)} %bitcast.16) | data formatting | bytes 1048576
  41.6 1.1 %copy.23 = f32[2,32,8,256]{3,2,1,0:T(8,128)} copy(f32[2,32,8,256]{3,1,2,0:T(8,128)S(1)} %bitcast.15) | data formatting | bytes 1048576
  (1 shorter events, 0.0 us)
Async XLA Ops:
  1.3 0.7 %copy-start.4 = (f32[32]{0:T(128)S(1)}, f32[32]{0:T(128)}, u32[]{:S(2)}) copy-start(f32[32]{0:T(128)} %param.13) | copy-start | bytes 388
  1.3 0.7 %copy-start.5 = (f32[32]{0:T(128)S(1)}, f32[32]{0:T(128)}, u32[]{:S(2)}) copy-start(f32[32]{0:T(128)} %param.14) | copy-start | bytes 388
  1.3 0.7 %copy-start.1 = (f32[32]{0:T(128)S(1)}, f32[32]{0:T(128)}, u32[]{:S(2)}) copy-start(f32[32]{0:T(128)} %param.10) | copy-start | bytes 388
  1.3 0.7 %copy-start.2 = (f32[32]{0:T(128)S(1)}, f32[32]{0:T(128)}, u32[]{:S(2)}) copy-start(f32[32]{0:T(128)} %param.11) | copy-start | bytes 388
  1.3 0.7 %copy-start.3 = (f32[32]{0:T(128)S(1)}, f32[32]{0:T(128)}, u32[]{:S(2)}) copy-start(f32[32]{0:T(128)} %param.12) | copy-start | bytes 388
  2.1 1.3 %copy-start = (f32[2,32,8,256]{3,2,1,0:T(8,128)S(1)}, f32[2,32,8,256]{3,2,1,0:T(8,128)}, u32[]{:S(2)}) copy-start(f32[2,32,8,256]{3,2,1,0:T(8,128)} %param.9) | copy-start | bytes 1572868

commit v3 on v2

--- a/solution.py
+++ b/solution.py
@@ -117,7 +117,12 @@
             local = jnp.clip(row - w * R, 0, R - 1)
             for f in range(2):
                 pick[k, e, f] = source[f, local]
-            tips[k, e] = ends(pick[k, e, 0], C)
+            x = ends(pick[k, e, 0], C)
+            folded = jnp.zeros((8, T), jnp.float32)
+            for part in range(K // 8):
+                turned = roll(x[8 * part:8 * part + 8], 2 * part + 1)
+                folded = jnp.where(lane[:8] // 2 == part, turned, folded)
+            tips[k, e] = folded
             send(pick.at[k, e], slots[k].at[w], s + w, {"wide": target}, cond)
             for d, dn in enumerate(steps):
                 send(
@@ -167,8 +172,9 @@
                 left = scale * sum(corners[k][0, owner] for k in ks)
                 if N > 2:
                     right = scale * sum(corners[k][1, owner] for k in ks)
-                    left = jnp.where(lane < T // 2, right, left)
-                dst[0, near, :, c:c + T] = left
+                    left = jnp.where(lane[:8] % 2 == 0, left, right)
+                for part in range(K // 8):
+                    dst[0, near, 8 * part:8 * part + 8, c:c + T] = roll(left, T - 1 - 2 * part)
             pl.when(w == target)(fill)
 
     def column_sums(ext, rows, out):
@@ -179,7 +185,7 @@
             return 0
         lax.fori_loop(0, rows + 2, body, 0, unroll=True)
 
-    def advance(ext, rows, lanes, mine, theirs, lap, f, g, store):
+    def advance(ext, rows, lanes, mine, theirs, lap, f, g, store, parts=1, after=None):
         L = lanes + T
         near = lambda x: roll(x, 1) + roll(x, L - 1)
 
@@ -211,7 +217,11 @@
             drift = drp * (0.5 * (qd - qu)) + dcp * (0.5 * (qr - ql))
             store(1, i, q1 + diffuse * lap_q - advect * drift)
             return 0
-        lax.fori_loop(0, rows, body, 0, unroll=True)
+        size = rows // parts
+        for part in range(parts):
+            lax.fori_loop(part * size, (part + 1) * size, body, 0, unroll=True)
+            if after:
+                after(part)
 
     def pack_nest(ref, start, dst, tile):
         dst[tile] = jnp.zeros((K, T), jnp.float32)
@@ -226,7 +236,6 @@
 
     pl.semaphore_wait(barrier, count + 1)
     wait_rows = [send_rows(p_ref, 0, pe, R, C), send_rows(n_ref, 0, ne, r, c)]
-    wait_old = send_picks(p_ref, 0)
     pack[0] = jnp.zeros((K, T), jnp.float32)
 
     def pack_parent(i, _):
@@ -241,6 +250,7 @@
         x = ends(p_ref[0, row], C)
         pack[1] = jnp.where(lane // 4 == slot, roll(x, 4 * slot + 2), pack[1])
     wait_packs = send_packs(pack, cr, 1)
+    wait_old = send_picks(p_ref, 0)
 
     for j in range(5):
         cb[j] = jnp.broadcast_to(cf_ref[:, j:j + 1], cb.shape[1:])
@@ -331,25 +341,39 @@
     column_sums(ne2, r, psm)
     wait_m = share(psm, prm)
     wait_m()
-    advance(ne2, r, c, psm, prm, ln, 2.0, 8.0, store_nest)
     narrower = jnp.where(
         lax.broadcasted_iota(jnp.int32, (c, C), 0) // 2
         == lax.broadcasted_iota(jnp.int32, (c, C), 1), 0.25, 0.0
     )
     base = w * half
-    for i in range(half):
-        for f in range(2):
-            cg[base + i, f] = jnp.dot(
-                no_ref[f, 2 * i] + no_ref[f, 2 * i + 1], narrower,
-                precision=lax.Precision.HIGHEST, preferred_element_type=jnp.float32,
-            )
-    s = take(W)
-    for dw in range(1, W):
-        block = cg.at[pl.ds(base, half)]
-        send(block, block, s + w, {"wide": lax.rem(w + dw, W)})
-    for dw in range(1, W):
-        src = lax.rem(w + dw, W)
-        receive(cg.at[pl.ds(src * half, half)], s + src)
+    pieces = 2 if half % 2 == 0 else 1
+    many = half // pieces
+    s_down, s_up = take(pieces * W), take(pieces * W)
+    block = lambda at, piece: cg.at[pl.ds(at * half + piece * many, many)]
+
+    def send_coarse(piece):
+        for i in range(piece * many, (piece + 1) * many):
+            for f in range(2):
+                cg[base + i, f] = jnp.dot(
+                    no_ref[f, 2 * i] + no_ref[f, 2 * i + 1], narrower,
+                    precision=lax.Precision.HIGHEST, preferred_element_type=jnp.float32,
+                )
+        own = block(w, piece)
+        for far in (2, 1):
+            send(own, own, s_down + piece * W + w, {"wide": w + far}, w + far < W)
+            send(own, own, s_up + piece * W + w, {"wide": w - far}, w - far >= 0)
+
+    advance(ne2, r, c, psm, prm, ln, 2.0, 8.0, store_nest, pieces, send_coarse)
+    for hop in (2, 1) + tuple(range(3, W)):
+        for piece in range(pieces):
+            for first, src, there, to, more in (
+                (s_down, jnp.maximum(w - hop, 0), w >= hop, down, below),
+                (s_up, jnp.minimum(w + hop, W - 1), w + hop < W, up, above),
+            ):
+                one, sem = block(src, piece), first + piece * W + src
+                receive(one, sem, there)
+                if 2 <= hop < W - 1:
+                    send(one, one, sem, to, there & more)
 
     def absorb(i, _):
         at = w * R + i - anchor
@@ -375,7 +399,7 @@
     F = lambda *dims: pltpu.VMEM(dims, jnp.float32)
     up8 = lambda x: -(-x // 8) * 8
     sums = lambda rows, lanes: F(up8(rows + 2), lanes + T)
-    nsem = 40 + 16 * D + 4 * W * (1 + D)
+    nsem = 64 + 24 * D + 4 * W * (3 + D)
     vm = pl.BlockSpec(memory_space=pltpu.VMEM)
     a, b = pl.pallas_call(
         functools.partial(kernel, W, N),
@@ -389,7 +413,7 @@
             F(R + 2, K, C + T), F(r + 2, K, c + T), F(5, K, max(C, c) + T),
             F(2, K, T), F(1, K, T), F(D, 3, 2, K, T), F(D, 3, 1, K, T),
             sums(R, C), sums(R, C), sums(r, c), sums(r, c), sums(r, c), sums(r, c),
-            F(2, 2, 2, K, C), F(2, 2, K, T), F(W, 2, K, C), F(W, 2, K, C), F(D, W, K, T), F(D, W, K, T),
+            F(2, 2, 2, K, C), F(2, 2, 8, T), F(W, 2, K, C), F(W, 2, K, C), F(D, W, 8, T), F(D, W, 8, T),
             F(W * (r // 2), 2, K, C),
             pltpu.SemaphoreType.DMA((nsem,)), pltpu.SemaphoreType.DMA((nsem,)),
         ],

time: 43.2 us -> 42.1 us (0.975)
  Pallas kernels: 37 us -> 36.2 us
    pallas_call x1, Pallas kernels: 37 us -> 36.2 us  [shards(): pl.pallas_call(functools.partial(kernel, W, N), out_shape=(jax.ShapeDtype...]
where the time goes in v3:
time: 42.1 us; the launch traced here: 41.9 us
  Pallas kernels  36.2 us (86%)
  local copies, waits for them, and re-layouts  4.41 us (10%)
  between operations  1.35 us (3%)
    pallas_call x1, Pallas kernels, shards(): pl.pallas_call(functools.partial(kernel, W, N), out_shape=(jax.ShapeDtype...  36.2 us
    unnamed x16, local copies, waits for them, and re-layouts  4.3 us

profile of v3, /device:TPU:0, one launch (start us, length us, event | category | flops | bytes accessed | tf_op | source)
XLA Modules:
  0.0 41.9 jit_solution(2828700466450193921)
XLA Ops:
  1.3 0.0 copy-start.4
  1.3 0.0 copy-start.5
  1.3 0.0 copy-start.1
  1.3 0.0 copy-start.2
  1.3 0.0 copy-start.3
  1.3 0.6 %copy-done.4 = f32[32]{0:T(128)S(1)} copy-done((f32[32]{0:T(128)S(1)}, f32[32]{0:T(128)}, u32[]{:S(2)}) %copy-start.4) | copy-done | bytes 152
  1.9 0.0 copy-done.5
  2.0 0.0 copy-done.1
  2.0 0.0 copy-done.2
  2.0 0.0 copy-done.3
  2.0 0.1 copy.21.cf_ref
  2.1 0.0 copy-start
  2.1 1.3 %copy.27 = f32[2,32,16,128]{3,1,2,0:T(8,128)S(1)} copy(f32[2,32,16,128]{3,2,1,0:T(8,128)} %param.8) | data formatting | bytes 1048576 | tf_op args[0]
  3.4 0.0 copy-done
  3.4 0.2 copy.26
  3.6 36.2 %shard_map.95 = (f32[2,16,32,128]{3,2,1,0:T(8,128)S(1)}, f32[2,8,32,256]{3,2,1,0:T(8,128)S(1)}) custom-call(s32[1]{0:T(128)S(6)} %copy.28.anchor_ref, f32[32,5]{1,0:T(8,128)S(1)} %copy.21.cf_ref, f32[2,16,32,128]{3,2,1,0:T(8,128)S(1)} %bitcast.13, f32[2,8,32,256]{3,2,1,0:T(8,128)S(1)} %bitcast.14), custom_call_target="tpu_custom_call" | custom-call | tf_op jit(solution)/shard_map/pallas_call | solution.py:404
  39.7 1.1 %copy.22 = f32[2,32,16,128]{3,2,1,0:T(8,128)} copy(f32[2,32,16,128]{3,1,2,0:T(8,128)S(1)} %bitcast.16) | data formatting | bytes 1048576
  40.8 1.1 %copy.23 = f32[2,32,8,256]{3,2,1,0:T(8,128)} copy(f32[2,32,8,256]{3,1,2,0:T(8,128)S(1)} %bitcast.15) | data formatting | bytes 1048576
  (1 shorter events, 0.0 us)
Async XLA Ops:
  1.3 0.7 %copy-start.4 = (f32[32]{0:T(128)S(1)}, f32[32]{0:T(128)}, u32[]{:S(2)}) copy-start(f32[32]{0:T(128)} %param.13) | copy-start | bytes 388
  1.3 0.7 %copy-start.5 = (f32[32]{0:T(128)S(1)}, f32[32]{0:T(128)}, u32[]{:S(2)}) copy-start(f32[32]{0:T(128)} %param.14) | copy-start | bytes 388
  1.3 0.7 %copy-start.1 = (f32[32]{0:T(128)S(1)}, f32[32]{0:T(128)}, u32[]{:S(2)}) copy-start(f32[32]{0:T(128)} %param.10) | copy-start | bytes 388
  1.3 0.7 %copy-start.2 = (f32[32]{0:T(128)S(1)}, f32[32]{0:T(128)}, u32[]{:S(2)}) copy-start(f32[32]{0:T(128)} %param.11) | copy-start | bytes 388
  1.3 0.7 %copy-start.3 = (f32[32]{0:T(128)S(1)}, f32[32]{0:T(128)}, u32[]{:S(2)}) copy-start(f32[32]{0:T(128)} %param.12) | copy-start | bytes 388
  2.1 1.3 %copy-start = (f32[2,32,8,256]{3,2,1,0:T(8,128)S(1)}, f32[2,32,8,256]{3,2,1,0:T(8,128)}, u32[]{:S(2)}) copy-start(f32[2,32,8,256]{3,2,1,0:T(8,128)} %param.9) | copy-start | bytes 1572868

commit v4 on v3

--- a/solution.py
+++ b/solution.py
@@ -234,8 +234,6 @@
             return 0
         lax.fori_loop(0, r, body, 0, unroll=True)
 
-    pl.semaphore_wait(barrier, count + 1)
-    wait_rows = [send_rows(p_ref, 0, pe, R, C), send_rows(n_ref, 0, ne, r, c)]
     pack[0] = jnp.zeros((K, T), jnp.float32)
 
     def pack_parent(i, _):
@@ -249,9 +247,6 @@
     for slot, row in ((2 * r, 0), (2 * r + 1, R - 1)):
         x = ends(p_ref[0, row], C)
         pack[1] = jnp.where(lane // 4 == slot, roll(x, 4 * slot + 2), pack[1])
-    wait_packs = send_packs(pack, cr, 1)
-    wait_old = send_picks(p_ref, 0)
-
     for j in range(5):
         cb[j] = jnp.broadcast_to(cf_ref[:, j:j + 1], cb.shape[1:])
     for f in range(2):
@@ -261,6 +256,11 @@
         def clear(first=first):
             pe[:, first:first + 2] = jnp.zeros((2, 2, K, C + T), jnp.float32)
         pl.when(cond)(clear)
+    pl.semaphore_wait(barrier, count + 1)
+    wait_rows = [send_rows(p_ref, 0, pe, R, C), send_rows(n_ref, 0, ne, r, c)]
+    wait_packs = send_packs(pack, cr, 1)
+    wait_old = send_picks(p_ref, 0)
+
     left_part = lane % 4 < 2
     side = lambda slot: lax.rem(2 * T - 2 - 4 * slot, T)
     wait_packs()

time: 42.1 us -> 42.1 us (level)
  no operation moved by 1% of the time
where the time goes in v4:
time: 42.1 us; the launch traced here: 41.9 us
  Pallas kernels  36.2 us (86%)
  local copies, waits for them, and re-layouts  4.41 us (10%)
  between operations  1.35 us (3%)
    pallas_call x1, Pallas kernels, shards(): pl.pallas_call(functools.partial(kernel, W, N), out_shape=(jax.ShapeDtype...  36.2 us
    unnamed x16, local copies, waits for them, and re-layouts  4.3 us

profile of v4, /device:TPU:0, one launch (start us, length us, event | category | flops | bytes accessed | tf_op | source)
XLA Modules:
  0.0 41.9 jit_solution(12906472152186821084)
XLA Ops:
  1.3 0.0 copy-start.4
  1.3 0.0 copy-start.5
  1.3 0.0 copy-start.1
  1.3 0.0 copy-start.2
  1.3 0.0 copy-start.3
  1.3 0.6 %copy-done.4 = f32[32]{0:T(128)S(1)} copy-done((f32[32]{0:T(128)S(1)}, f32[32]{0:T(128)}, u32[]{:S(2)}) %copy-start.4) | copy-done | bytes 152
  1.9 0.0 copy-done.5
  2.0 0.0 copy-done.1
  2.0 0.0 copy-done.2
  2.0 0.0 copy-done.3
  2.0 0.1 copy.21.cf_ref
  2.1 0.0 copy-start
  2.1 1.3 %copy.27 = f32[2,32,16,128]{3,1,2,0:T(8,128)S(1)} copy(f32[2,32,16,128]{3,2,1,0:T(8,128)} %param.8) | data formatting | bytes 1048576 | tf_op args[0]
  3.4 0.0 copy-done
  3.4 0.2 copy.26
  3.6 36.2 %shard_map.95 = (f32[2,16,32,128]{3,2,1,0:T(8,128)S(1)}, f32[2,8,32,256]{3,2,1,0:T(8,128)S(1)}) custom-call(s32[1]{0:T(128)S(6)} %copy.28.anchor_ref, f32[32,5]{1,0:T(8,128)S(1)} %copy.21.cf_ref, f32[2,16,32,128]{3,2,1,0:T(8,128)S(1)} %bitcast.13, f32[2,8,32,256]{3,2,1,0:T(8,128)S(1)} %bitcast.14), custom_call_target="tpu_custom_call" | custom-call | tf_op jit(solution)/shard_map/pallas_call | solution.py:404
  39.7 1.1 %copy.22 = f32[2,32,16,128]{3,2,1,0:T(8,128)} copy(f32[2,32,16,128]{3,1,2,0:T(8,128)S(1)} %bitcast.16) | data formatting | bytes 1048576
  40.8 1.1 %copy.23 = f32[2,32,8,256]{3,2,1,0:T(8,128)} copy(f32[2,32,8,256]{3,1,2,0:T(8,128)S(1)} %bitcast.15) | data formatting | bytes 1048576
  (1 shorter events, 0.0 us)
Async XLA Ops:
  1.3 0.7 %copy-start.4 = (f32[32]{0:T(128)S(1)}, f32[32]{0:T(128)}, u32[]{:S(2)}) copy-start(f32[32]{0:T(128)} %param.13) | copy-start | bytes 388
  1.3 0.7 %copy-start.5 = (f32[32]{0:T(128)S(1)}, f32[32]{0:T(128)}, u32[]{:S(2)}) copy-start(f32[32]{0:T(128)} %param.14) | copy-start | bytes 388
  1.3 0.7 %copy-start.1 = (f32[32]{0:T(128)S(1)}, f32[32]{0:T(128)}, u32[]{:S(2)}) copy-start(f32[32]{0:T(128)} %param.10) | copy-start | bytes 388
  1.3 0.7 %copy-start.2 = (f32[32]{0:T(128)S(1)}, f32[32]{0:T(128)}, u32[]{:S(2)}) copy-start(f32[32]{0:T(128)} %param.11) | copy-start | bytes 388
  1.3 0.7 %copy-start.3 = (f32[32]{0:T(128)S(1)}, f32[32]{0:T(128)}, u32[]{:S(2)}) copy-start(f32[32]{0:T(128)} %param.12) | copy-start | bytes 388
  2.1 1.3 %copy-start = (f32[2,32,8,256]{3,2,1,0:T(8,128)S(1)}, f32[2,32,8,256]{3,2,1,0:T(8,128)}, u32[]{:S(2)}) copy-start(f32[2,32,8,256]{3,2,1,0:T(8,128)} %param.9) | copy-start | bytes 1572868
